TPU v7x, 32 devices: a whole 2x2x4 slice. The times are simulated.
32 devices in a mesh: section: 4 (over y, core), dom: 8 (over z, x).
Axes of the slice: x: 2, y: 2, z: 4, core: 2. Of those that a mesh axis runs over, the one named last changes fastest.
Arguments:
- right_sides: float32 [256, 32, 128], P(('section', 'dom')), may hold values from -6 to 6
- diag_inverse: bfloat16 [256, 128, 128], P(('section', 'dom')), as said below
- diag_blocks: bfloat16 [256, 128, 128], P(('section', 'dom')), as said below
- lower_blocks: bfloat16 [256, 3, 128, 128], P(('section', 'dom'))
- upper_blocks: bfloat16 [256, 3, 128, 128], P(('section', 'dom'))
- halo_blocks: bfloat16 [256, 2, 128, 128], P(('section', 'dom')), may hold values from -0.1875 to 0.1875
- lower_index: int32 [256, 3], P(('section', 'dom')), may hold values from 0 to 7, as said below
- upper_index: int32 [256, 3], P(('section', 'dom')), may hold values from 0 to 7, as said below
- halo_index: int32 [256, 2], P(('section', 'dom')), may hold values from 0 to 7, as said below
Outputs:
- solution: float32 [256, 32, 128], P(('section', 'dom'))
- product: float32 [256, 32, 128], P(('section', 'dom'))
Inputs may be any that keep to these rules, and one draw needn't show every extreme that they name: `lower_index`: for block row g with k = g mod 8, every entry lies in 0 to k, and the first entry equals k. `upper_index`: for block row g with k = g mod 8, every entry lies in k to 7, and the first entry equals k. `halo_index`: for block row g the first entry equals g mod 8. `diag_inverse`: each block is the identity scaled row by row plus a full block. `diag_blocks`: each block is the identity scaled row by row plus a full block.
All inputs are finite; a program needn't handle non-finite values.
Results may differ from a plain program's by a relative error of at most 0.029.
Values may be sent and summed in bfloat16 or wider, within the bound.
No kernel may reach another device: no remote copies, remote signals or barrier semaphores. Data moves between devices by JAX's collectives and lax.ppermute only.
A program may use at most 64 MiB of HBM per device.

v0:
```python
import jax
import jax.numpy as jnp
from jax import lax
from jax.sharding import PartitionSpec as P

RIM = 4


highest = lax.Precision.HIGHEST


def prefix_2(shard, axis, combine, identity):
    length, index = (lax.axis_size(axis), lax.axis_index(axis))
    everything = jax.tree.map(
        lambda part, kind: lax.all_gather(part.astype(kind), axis),
        shard,
        (jnp.bfloat16, jnp.bfloat16),
    )
    start = jax.tree.map(
        lambda part, zero: jnp.broadcast_to(jnp.asarray(zero, part.dtype), part.shape),
        shard,
        identity,
    )

    def prefix_step(k, before):
        reached = k < index
        new = combine(
            before, jax.tree.map(lambda part, own: part[k].astype(own.dtype), everything, shard)
        )
        return jax.tree.map(lambda a, b: jnp.where(reached, a, b), new, before)

    return lax.fori_loop(0, length, prefix_step, start)


def entering(shard, axis, combine, identity):
    length, index = (lax.axis_size(axis), lax.axis_index(axis))
    everything = jax.tree.map(
        lambda part, kind: lax.all_gather(part.astype(kind), axis),
        shard,
        jax.tree.map(lambda a: jnp.bfloat16 if a.dtype == jnp.float32 else a.dtype, shard),
    )
    start = jax.tree.map(
        lambda part, zero: jnp.broadcast_to(jnp.asarray(zero, part.dtype), part.shape),
        shard,
        identity,
    )

    def entering_step(k, before):
        at = length - 1 - k
        reached = at > index
        new = combine(
            before, jax.tree.map(lambda part, own: part[at].astype(own.dtype), everything, shard)
        )
        return jax.tree.map(lambda a, b: jnp.where(reached, a, b), new, before)

    return lax.fori_loop(0, length, entering_step, start)


def extended(block, sides, width):
    for axis, dim in sides:
        count = lax.axis_size(axis)
        forward = [(i, i + 1) for i in range(count - 1)]
        backward = [(target, source) for source, target in forward]
        low = lax.ppermute(
            lax.slice_in_dim(block, block.shape[dim] - width, None, axis=dim), axis, forward
        )
        high = lax.ppermute(lax.slice_in_dim(block, 0, width, axis=dim), axis, backward)
        block = jnp.concatenate([low, block, high], axis=dim)
    return block


def select_rows(pointers, first, candidates):
    offsets = jnp.arange(candidates.shape[0], dtype=jnp.int32) + first
    weights = (pointers[:, None] == offsets[None, :]).astype(jnp.bfloat16)
    picked = jnp.einsum("sr,rqb->sqb", weights, candidates, preferred_element_type=jnp.float32)
    return picked.astype(jnp.bfloat16)


def solve_down(target, inverse, lower_part, pointers, inflow):
    solved_rows = []
    narrow_rows = []
    inflow_narrow = inflow.astype(jnp.bfloat16)
    for position in range(target.shape[0]):
        candidates = jnp.stack(narrow_rows + [inflow_narrow], axis=0)
        source = select_rows(pointers[position], 0, candidates)
        summed = jnp.einsum(
            "sqb,sbc->qc", source, lower_part[position], preferred_element_type=jnp.float32
        )
        gap = (target[position] - summed).astype(jnp.bfloat16)
        result = jnp.dot(gap, inverse[position], preferred_element_type=jnp.float32)
        solved_rows.append(result)
        narrow_rows.append(result.astype(jnp.bfloat16))
    return jnp.stack(solved_rows, axis=0)


def solve_up(target, inverse, upper_part, pointers, inflow):
    count = target.shape[0]
    solved_rows = []
    narrow_rows = []
    inflow_narrow = inflow.astype(jnp.bfloat16)
    for position in range(count - 1, -1, -1):
        candidates = jnp.stack([inflow_narrow] + narrow_rows, axis=0)
        source = select_rows(pointers[position], position, candidates)
        summed = jnp.einsum(
            "sqb,sbc->qc", source, upper_part[position], preferred_element_type=jnp.float32
        )
        result = target[position] - jnp.dot(
            summed.astype(jnp.bfloat16), inverse[position], preferred_element_type=jnp.float32
        )
        solved_rows.insert(0, result)
        narrow_rows.insert(0, result.astype(jnp.bfloat16))
    return jnp.stack(solved_rows, axis=0)


def apply_rows(
    rounded,
    diag_part,
    lower_part,
    lower_pointers,
    upper_part,
    upper_pointers,
    halo_part,
    halo_pointers,
    before,
    after,
    rim_rows,
):
    positions = jnp.arange(rounded.shape[0], dtype=jnp.int32)[:, None]
    lower_source = jnp.where(
        (lower_pointers == positions)[:, :, None, None],
        before[None, None],
        jnp.take(rounded, lower_pointers, axis=0),
    )
    upper_source = jnp.where(
        (upper_pointers == positions)[:, :, None, None],
        after[None, None],
        jnp.take(rounded, upper_pointers, axis=0),
    )
    halo_source = jnp.take(rim_rows, halo_pointers, axis=0)
    total = jnp.einsum("rqb,rbc->rqc", rounded, diag_part, preferred_element_type=jnp.float32)
    total = total + jnp.einsum(
        "rsqb,rsbc->rqc", lower_source, lower_part, preferred_element_type=jnp.float32
    )
    total = total + jnp.einsum(
        "rsqb,rsbc->rqc", upper_source, upper_part, preferred_element_type=jnp.float32
    )
    total = total + jnp.einsum(
        "rsqb,rsbc->rqc", halo_source, halo_part, preferred_element_type=jnp.float32
    )
    return total


def compose(earlier, later):
    mapping = jnp.dot(earlier[0], later[0], precision=highest)
    offset = jnp.dot(earlier[1], later[0], precision=highest) + later[1]
    return (mapping, offset)


def on_device(
    right_sides,
    diag_inverse,
    diag_blocks,
    lower_blocks,
    upper_blocks,
    halo_blocks,
    lower_index,
    upper_index,
    halo_index,
):
    local_rows = right_sides.shape[0]
    count_rhs = right_sides.shape[1]
    width = right_sides.shape[2]
    inflow_zero = jnp.zeros((count_rhs, width), jnp.float32)
    basis = jnp.eye(width, dtype=jnp.float32)
    seeds = jnp.concatenate([inflow_zero, basis], axis=0)
    padding = jnp.zeros((local_rows, width, width), jnp.float32)
    joint = solve_down(
        jnp.concatenate([right_sides, padding], axis=1),
        diag_inverse,
        lower_blocks,
        lower_index,
        seeds,
    )
    base = joint[:, :count_rhs]
    response = joint[:, count_rhs:]
    prefix = prefix_2((response[-1], base[-1]), "section", compose, (basis, inflow_zero))
    forward = base + jnp.einsum("qb,rbc->rqc", prefix[1], response, precision=highest)
    joint = solve_up(
        jnp.concatenate([forward, padding], axis=1), diag_inverse, upper_blocks, upper_index, seeds
    )
    base = joint[:, :count_rhs]
    response = joint[:, count_rhs:]
    suffix = entering((response[0], base[0]), "section", compose, (basis, inflow_zero))
    solution = base + jnp.einsum("qb,rbc->rqc", suffix[1], response, precision=highest)
    rounded = solution.astype(jnp.bfloat16)
    padded = extended(rounded, (("section", 0),), 1)
    widened = extended(rounded, (("dom", 0),), RIM)
    rim_rows = jnp.concatenate([widened[:RIM], widened[widened.shape[0] - RIM :]], axis=0)
    product = apply_rows(
        rounded,
        diag_blocks,
        lower_blocks,
        lower_index,
        upper_blocks,
        upper_index,
        halo_blocks,
        halo_index,
        padded[0],
        padded[-1],
        rim_rows,
    )
    return (solution, product)


def solution(mesh):
    in_specs = (
        P(("section", "dom"), None, None),
        P(("section", "dom"), None, None),
        P(("section", "dom"), None, None),
        P(("section", "dom"), None, None, None),
        P(("section", "dom"), None, None, None),
        P(("section", "dom"), None, None, None),
        P(("section", "dom"), None),
        P(("section", "dom"), None),
        P(("section", "dom"), None),
    )
    out_specs = (P(("section", "dom"), None, None), P(("section", "dom"), None, None))
    return jax.shard_map(
        on_device, mesh=mesh, in_specs=in_specs, out_specs=out_specs, check_vma=False
    )
```

profile of v0, /device:TPU:17, one launch (start us, length us, event | category | flops | bytes accessed | tf_op | source)
XLA Modules:
  0.0 82.4 jit_solution(17099026824534652256)
XLA Ops:
  0.7 0.7 copy-done.13
  1.8 1.2 %constant_dynamic-update-slice_fusion.33 = (f32[8,160,128]{2,1,0:T(8,128)S(1)}, bf16[160,128]{1,0:T(8,128)(2,1)S(1)}) fusion(bf16[8,128,128]{2,1,0:T(8,128)(2,1)} %param.16, f32[160,128]{1,0:T(8,128)S(1)} %get-tuple-element.342, f32[3]{0:T(128)S(1)} %convert_reduce_fusion.1, bf16[8,3,128,128]{3,2,1,0:T(8,128)(2,1)} %param.18, f32[8,32,128]{2,1,0:T(8,128)S(1)} %copy-done.1), kind=kOutput, calls=%fused_computation.177 | convolution fusion | flops 21155840 | bytes 466956 | tf_op jit(solution)/shard_map/dot_general | solution.py:90
  5.6 1.0 %convolution_convert_fusion.12 = bf16[3,160,128]{2,0,1:T(4,128)(2,1)} fusion(bf16[3,160,128]{2,1,0:T(8,128)(2,1)S(1)} %pad_maximum_fusion.2, s32[3]{0:T(128)S(1)} %get-tuple-element.279), kind=kOutput, calls=%fused_computation.51 | convolution fusion | flops 430089 | bytes 245772 | tf_op jit(solution)/shard_map/sr,rqb->sqb/dot_general | solution.py:75
  6.6 1.2 %constant_dynamic-update-slice_fusion.31 = (f32[8,160,128]{2,1,0:T(8,128)S(1)}, bf16[160,128]{1,0:T(8,128)(2,1)S(1)}) fusion(f32[8,160,128]{2,1,0:T(8,128)S(1)} %get-tuple-element.354, bf16[8,128,128]{2,1,0:T(8,128)(2,1)S(1)} %copy-done.4, bf16[3,160,128]{2,0,1:T(4,128)(2,1)} %convolution_convert_fusion.12, bf16[8,3,128,128]{3,2,1,0:T(8,128)(2,1)S(1)} %copy-done.3, ...), kind=kOutput, calls=%fused_computation.175 | convolution fusion | flops 21032960 | bytes 507904 | tf_op jit(solution)/shard_map/dot_general | solution.py:90
  8.4 1.0 %convolution_convert_fusion.11 = bf16[3,160,128]{2,0,1:T(4,128)(2,1)} fusion(bf16[4,160,128]{2,1,0:T(8,128)(2,1)S(1)} %pad_maximum_fusion, s32[3]{0:T(128)S(1)} %get-tuple-element.278), kind=kOutput, calls=%fused_computation.50 | convolution fusion | flops 552972 | bytes 286732 | tf_op jit(solution)/shard_map/sr,rqb->sqb/dot_general | solution.py:75
  9.4 1.9 %constant_dynamic-update-slice_fusion.22 = (bf16[8,160,128]{2,1,0:T(8,128)(2,1)}, bf16[160,128]{1,0:T(8,128)(2,1)S(1)}, f32[160,128]{1,0:T(8,128)}) fusion(bf16[8,160,128]{2,1,0:T(8,128)(2,1)} %get-tuple-element.305, bf16[8,128,128]{2,1,0:T(8,128)(2,1)S(1)} %copy-done.4, bf16[3,160,128]{2,0,1:T(4,128)(2,1)} %convolution_convert_fusion.11, ...), kind=kOutput, calls=%fused_computation.166 | convolution fusion | flops 21032960 | bytes 589824 | tf_op jit(solution)/shard_map/dot_general | solution.py:90
  11.7 1.0 %constant_dynamic-update-slice_fusion.21 = (bf16[8,160,128]{2,1,0:T(8,128)(2,1)}, bf16[7,160,128]{2,1,0:T(8,128)(2,1)S(1)}, bf16[6,160,128]{2,1,0:T(8,128)(2,1)S(1)}, f32[160,128]{1,0:T(8,128)}) fusion(bf16[8,160,128]{2,1,0:T(8,128)(2,1)} %get-tuple-element.303, bf16[7,160,128]{2,1,0:T(8,128)(2,1)S(1)} %get-tuple-element.324, ...), kind=kOutput, calls=%fused_computation.165 | convolution fusion | flops 21032960 | bytes 630784 | tf_op jit(solution)/shard_map/dot_general | solution.py:90
  13.6 0.9 %constant_dynamic-update-slice_fusion.20 = (bf16[8,160,128]{2,1,0:T(8,128)(2,1)S(1)}, bf16[7,160,128]{2,1,0:T(8,128)(2,1)S(1)}, f32[160,128]{1,0:T(8,128)}) fusion(bf16[8,160,128]{2,1,0:T(8,128)(2,1)S(1)} %copy-done.7, bf16[7,160,128]{2,1,0:T(8,128)(2,1)S(1)} %get-tuple-element.318, bf16[8,128,128]{2,1,0:T(8,128)(2,1)S(1)} %copy-done.4, ...), kind=kOutput, calls=%fused_computation.164 | convolution fusion | flops 21032960 | bytes 589824 | tf_op jit(solution)/shard_map/dot_general | solution.py:90
  15.2 0.7 constant_dynamic-update-slice_fusion.18
  16.1 0.9 %copy-done.8 = f32[160,128]{1,0:T(8,128)S(1)} copy-done((f32[160,128]{1,0:T(8,128)S(1)}, f32[160,128]{1,0:T(8,128)}, u32[]{:S(2)}) %copy-start.8) | copy-done | bytes 81944
  17.0 0.9 %copy-done.11 = f32[160,128]{1,0:T(8,128)S(1)} copy-done((f32[160,128]{1,0:T(8,128)S(1)}, f32[160,128]{1,0:T(8,128)}, u32[]{:S(2)}) %copy-start.11) | copy-done | bytes 81944
  18.5 0.8 copy-done.5
  19.3 0.7 copy-done.15
  20.2 0.8 slice_reduce_fusion.6
  21.6 6.0 %all_gather.16 = bf16[4,128,128]{2,1,0:T(8,128)(2,1)S(1)} all-gather(bf16[1,128,128]{2,1,0:T(8,128)(2,1)S(1)} %slice.300), channel_id=1, replica_groups=mesh['section'=4,'dom'=8] {'section'}, dimensions={0}, use_global_device_ids=true | all-gather | bytes 163840 | tf_op jit(solution)/shard_map/all_gather | solution.py:15
  27.6 5.2 %all_gather.17 = bf16[4,32,128]{2,1,0:T(8,128)(2,1)S(1)} all-gather(bf16[1,32,128]{2,1,0:T(8,128)(2,1)S(1)} %slice.301), channel_id=1, replica_groups=mesh['section'=4,'dom'=8] {'section'}, dimensions={0}, use_global_device_ids=true | all-gather | bytes 40960 | tf_op jit(solution)/shard_map/all_gather | solution.py:15
  32.8 0.7 while.30
  33.4 1.5 %fusion.19 = f32[8,32,128]{2,1,0:T(8,128)S(1)} fusion(f32[8,160,128]{2,1,0:T(8,128)} %copy-done.5, f32[32,128]{1,0:T(8,128)S(1)} %get-tuple-element.229), kind=kOutput, calls=%fused_computation.59 | convolution fusion | flops 50364416 | bytes 802816 | tf_op jit(solution)/shard_map/qb,rbc->rqc/dot_general | solution.py:187
  36.9 0.9 %constant_dynamic-update-slice_fusion.37 = (bf16[5,160,128]{2,1,0:T(8,128)(2,1)S(1)}, bf16[160,128]{1,0:T(8,128)(2,1)S(1)}, f32[160,128]{1,0:T(8,128)}) fusion(bf16[5,160,128]{2,1,0:T(8,128)(2,1)S(1)} %get-tuple-element.337, bf16[8,128,128]{2,1,0:T(8,128)(2,1)S(1)} %copy-done.4, bf16[3,160,128]{2,0,1:T(4,128)(2,1)S(1)} %convolution_convert_fusion.4, ...), kind=kOutput, calls=%fused_computation.181 | convolution fusion | flops 21032960 | bytes 589824 | tf_op jit(solution)/shard_map/dot_general | solution.py:107
  38.9 0.9 %constant_dynamic-update-slice_fusion.50 = (bf16[7,160,128]{2,1,0:T(8,128)(2,1)}, f32[160,128]{1,0:T(8,128)S(1)}) fusion(bf16[7,160,128]{2,1,0:T(8,128)(2,1)} %get-tuple-element.339, bf16[8,128,128]{2,1,0:T(8,128)(2,1)S(1)} %copy-done.4, bf16[3,160,128]{2,0,1:T(4,128)(2,1)S(1)} %convolution_convert_fusion.2, bf16[8,3,128,128]{3,2,1,0:T(8,128)(2,1)S(1)} %copy-done.2, ...), kind=kOutput, calls=%fused_computation.194 | convolution fusion | flops 21032960 | bytes 548864 | tf_op jit(solution)/shard_map/dot_general | solution.py:107
  43.0 1.3 %convolution_convert_fusion.1 = bf16[3,160,128]{2,0,1:T(4,128)(2,1)S(1)} fusion(bf16[7,160,128]{2,1,0:T(8,128)(2,1)} %constant_dynamic-update-slice_fusion.45, s32[7]{0:T(128)S(1)} %copy-done.20, s32[3]{0:T(128)S(1)} %copy-done.18), kind=kOutput, calls=%fused_computation.40 | convolution fusion | flops 921621 | bytes 409640 | tf_op jit(solution)/shard_map/sr,rqb->sqb/dot_general | solution.py:75
  45.6 0.9 %fusion.302 = (bf16[1,160,128]{2,1,0:T(8,128)(2,1)S(1)}, f32[8,160,128]{2,1,0:T(8,128)}) fusion(bf16[8,128,128]{2,1,0:T(8,128)(2,1)S(1)} %copy-done.4, bf16[3,160,128]{2,0,1:T(4,128)(2,1)S(1)} %convolution_convert_fusion, bf16[8,3,128,128]{3,2,1,0:T(8,128)(2,1)S(1)} %copy-done.2, f32[8,32,128]{2,1,0:T(8,128)S(1)} %fusion.19), kind=kOutput, calls=%fused_computation.431 | convolution fusion | flops 21032960 | bytes 548864 | tf_op jit(solution)/shard_map/dot_general | solution.py:107
  51.3 5.4 %all_gather.18 = bf16[4,128,128]{2,1,0:T(8,128)(2,1)S(1)} all-gather(bf16[1,128,128]{2,1,0:T(8,128)(2,1)S(1)} %slice.304), channel_id=1, replica_groups=mesh['section'=4,'dom'=8] {'section'}, dimensions={0}, use_global_device_ids=true | all-gather | bytes 163840 | tf_op jit(solution)/shard_map/all_gather | solution.py:38
  56.7 5.2 %all_gather.19 = bf16[4,32,128]{2,1,0:T(8,128)(2,1)S(1)} all-gather(bf16[1,32,128]{2,1,0:T(8,128)(2,1)S(1)} %slice.305), channel_id=1, replica_groups=mesh['section'=4,'dom'=8] {'section'}, dimensions={0}, use_global_device_ids=true | all-gather | bytes 40960 | tf_op jit(solution)/shard_map/all_gather | solution.py:38
  61.9 0.7 while.31
  62.6 2.2 %fusion.356 = (bf16[8,32,128]{2,1,0:T(8,128)(2,1)S(1)}, f32[8,32,128]{2,1,0:T(8,128)}) fusion(f32[32,128]{1,0:T(8,128)S(1)} %get-tuple-element.230, f32[8,160,128]{2,1,0:T(8,128)} %constant_dynamic-update-slice_fusion.60), kind=kOutput, calls=%fused_computation.435 | convolution fusion | flops 50397184 | bytes 868352 | tf_op jit(solution)/shard_map/qb,rbc->rqc/dot_general | solution.py:194
  64.7 2.1 %collective-permute-start.1 = (bf16[1,32,128]{2,1,0:T(8,128)(2,1)S(1)}, bf16[1,32,128]{2,1,0:T(8,128)(2,1)S(1)}, u32[]{:S(2)}, u32[]{:S(2)}) collective-permute-start(bf16[1,32,128]{2,1,0:T(8,128)(2,1)S(1)} %get-tuple-element.321), channel_id=1, source_target_pairs={{8,0},{16,8},{24,16},{9,1},{17,9},{25,17},{10,2},{18,10},{26,18},{... | collective-permute-start | bytes 24584 | tf_op jit(solution)/shard_map/ppermute | solution.py:67
  66.9 3.1 %collective-permute-start.2 = (bf16[4,32,128]{2,1,0:T(8,128)(2,1)S(1)}, bf16[4,32,128]{2,1,0:T(8,128)(2,1)S(1)}, u32[]{:S(2)}, u32[]{:S(2)}) collective-permute-start(bf16[4,32,128]{2,1,0:T(8,128)(2,1)S(1)} %get-tuple-element.322), channel_id=1, source_target_pairs={{0,1},{1,2},{2,3},{3,4},{4,5},{5,6},{6,7},{8,9},{9,10},{10,11},{11... | collective-permute-start | bytes 98312 | tf_op jit(solution)/shard_map/ppermute | solution.py:64
  70.0 3.1 %collective-permute-start.3 = (bf16[4,32,128]{2,1,0:T(8,128)(2,1)S(1)}, bf16[4,32,128]{2,1,0:T(8,128)(2,1)S(1)}, u32[]{:S(2)}, u32[]{:S(2)}) collective-permute-start(bf16[4,32,128]{2,1,0:T(8,128)(2,1)S(1)} %get-tuple-element.323), channel_id=1, source_target_pairs={{1,0},{2,1},{3,2},{4,3},{5,4},{6,5},{7,6},{9,8},{10,9},{11,10},{12... | collective-permute-start | bytes 98312 | tf_op jit(solution)/shard_map/ppermute | solution.py:67
  73.1 4.0 %collective-permute-start = (bf16[1,32,128]{2,1,0:T(8,128)(2,1)S(1)}, bf16[1,32,128]{2,1,0:T(8,128)(2,1)S(1)}, u32[]{:S(2)}, u32[]{:S(2)}) collective-permute-start(bf16[1,32,128]{2,1,0:T(8,128)(2,1)S(1)} %get-tuple-element.320), channel_id=1, source_target_pairs={{0,8},{8,16},{16,24},{1,9},{9,17},{17,25},{2,10},{10,18},{18,26},{... | collective-permute-start | bytes 24584 | tf_op jit(solution)/shard_map/ppermute | solution.py:64
  77.2 0.7 copy-done.19
  81.4 1.0 %fusion.22 = f32[8,32,128]{2,1,0:T(8,128)} fusion(f32[8,32,128]{2,1,0:T(8,128)S(1)} %convolution_bitcast_fusion.2, f32[8,32,128]{2,1,0:T(8,128)S(1)} %convolution_bitcast_fusion.3, f32[8,32,128]{2,1,0:T(8,128)S(1)} %fusion.357, bf16[8,3,128,128]{3,2,1,0:T(8,128)(2,1)S(1)} %copy-done.3, bf16[8,3,32,128]{3,2,1,0:T(8,128)(2,1)S(1)} %bitcast.618, ...), kind=kOutput, calls=%fused_computation.62 | convolution fusion | flops 25460736 | bytes 1515568 | tf_op jit(solution)/shard_map/rsqb,rsbc->rqc/dot_general | solution.py:141
  (167 shorter events, 24.1 us)
Async XLA Ops:
  0.6 80.5 %copy-start = (bf16[8,2,128,128]{3,2,1,0:T(8,128)(2,1)S(1)}, bf16[8,2,128,128]{3,2,1,0:T(8,128)(2,1)}, u32[]{:S(2)}) copy-start(bf16[8,2,128,128]{3,2,1,0:T(8,128)(2,1)} %param.20) | copy-start | bytes 1572868
  0.6 0.7 copy-start.13
  0.7 1.2 %copy-start.1 = (f32[8,32,128]{2,1,0:T(8,128)S(1)}, f32[8,32,128]{2,1,0:T(8,128)}, u32[]{:S(2)}) copy-start(f32[8,32,128]{2,1,0:T(8,128)} %param.15) | copy-start | bytes 393220
  0.7 3.3 %copy-start.3 = (bf16[8,3,128,128]{3,2,1,0:T(8,128)(2,1)S(1)}, bf16[8,3,128,128]{3,2,1,0:T(8,128)(2,1)}, u32[]{:S(2)}) copy-start(bf16[8,3,128,128]{3,2,1,0:T(8,128)(2,1)} %param.18) | copy-start | bytes 2359300
  3.7 0.9 %copy-start.4 = (bf16[8,128,128]{2,1,0:T(8,128)(2,1)S(1)}, bf16[8,128,128]{2,1,0:T(8,128)(2,1)}, u32[]{:S(2)}) copy-start(bf16[8,128,128]{2,1,0:T(8,128)(2,1)} %param.16) | copy-start | bytes 786436
  12.6 1.0 %copy-start.7 = (bf16[8,160,128]{2,1,0:T(8,128)(2,1)S(1)}, bf16[8,160,128]{2,1,0:T(8,128)(2,1)}, u32[]{:S(2)}) copy-start(bf16[8,160,128]{2,1,0:T(8,128)(2,1)} %get-tuple-element.317) | copy-start | bytes 983044
  15.2 0.9 %copy-start.10 = (f32[160,128]{1,0:T(8,128)S(1)}, f32[160,128]{1,0:T(8,128)}, u32[]{:S(2)}) copy-start(f32[160,128]{1,0:T(8,128)} %get-tuple-element.347) | copy-start | bytes 245764
  16.1 0.9 %copy-start.8 = (f32[160,128]{1,0:T(8,128)S(1)}, f32[160,128]{1,0:T(8,128)}, u32[]{:S(2)}) copy-start(f32[160,128]{1,0:T(8,128)} %get-tuple-element.348) | copy-start | bytes 245764
  17.0 0.9 %copy-start.11 = (f32[160,128]{1,0:T(8,128)S(1)}, f32[160,128]{1,0:T(8,128)}, u32[]{:S(2)}) copy-start(f32[160,128]{1,0:T(8,128)} %get-tuple-element.349) | copy-start | bytes 245764
  18.5 0.8 %copy-start.5 = (f32[8,160,128]{2,1,0:T(8,128)}, f32[8,160,128]{2,1,0:T(8,128)S(1)}, u32[]{:S(2)}) copy-start(f32[8,160,128]{2,1,0:T(8,128)S(1)} %get-tuple-element.314) | copy-start | bytes 1966084
  19.3 0.7 copy-start.15
  21.5 13.4 %copy-start.2 = (bf16[8,3,128,128]{3,2,1,0:T(8,128)(2,1)S(1)}, bf16[8,3,128,128]{3,2,1,0:T(8,128)(2,1)}, u32[]{:S(2)}) copy-start(bf16[8,3,128,128]{3,2,1,0:T(8,128)(2,1)} %param.19) | copy-start | bytes 2359300
  41.7 1.2 %copy-start.18 = (s32[3]{0:T(128)S(1)}, s32[3]{0:T(128)}, u32[]{:S(2)}) copy-start(s32[3]{0:T(128)} %get-tuple-element.273) | copy-start | bytes 40
  41.7 1.2 %copy-start.20 = (s32[7]{0:T(128)S(1)}, s32[7]{0:T(128)}, u32[]{:S(2)}) copy-start(s32[7]{0:T(128)} %iota_add_fusion.5) | copy-start | bytes 88
  42.3 1.9 %copy-start.6 = (bf16[8,160,128]{2,1,0:T(8,128)(2,1)S(1)}, bf16[8,160,128]{2,1,0:T(8,128)(2,1)}, u32[]{:S(2)}) copy-start(bf16[8,160,128]{2,1,0:T(8,128)(2,1)} %get-tuple-element.340) | copy-start | bytes 983044
  44.7 0.7 copy-start.17
  47.8 0.9 %copy-start.9 = (f32[160,128]{1,0:T(8,128)S(1)}, f32[160,128]{1,0:T(8,128)}, u32[]{:S(2)}) copy-start(f32[160,128]{1,0:T(8,128)} %get-tuple-element.358) | copy-start | bytes 245764
  62.5 15.8 %copy-start.12 = (bf16[8,128,128]{2,1,0:T(8,128)(2,1)S(1)}, bf16[8,128,128]{2,1,0:T(8,128)(2,1)}, u32[]{:S(2)}) copy-start(bf16[8,128,128]{2,1,0:T(8,128)(2,1)} %param.17) | copy-start | bytes 786436
  64.7 15.5 %collective-permute-start.1 = (bf16[1,32,128]{2,1,0:T(8,128)(2,1)S(1)}, bf16[1,32,128]{2,1,0:T(8,128)(2,1)S(1)}, u32[]{:S(2)}, u32[]{:S(2)}) collective-permute-start(bf16[1,32,128]{2,1,0:T(8,128)(2,1)S(1)} %get-tuple-element.321), channel_id=1, source_target_pairs={{8,0},{16,8},{24,16},{9,1},{17,9},{25,17},{10,2},{18,10},{26,18},{... | collective-permute-start | bytes 24584 | tf_op jit(solution)/shard_map/ppermute | solution.py:67
  66.8 10.3 %copy-start.14 = (s32[8,3]{0,1:T(4,128)S(1)}, s32[8,3]{0,1:T(4,128)}, u32[]{:S(2)}) copy-start(s32[8,3]{0,1:T(4,128)} %param.21) | copy-start | bytes 292
  66.9 13.7 %collective-permute-start.2 = (bf16[4,32,128]{2,1,0:T(8,128)(2,1)S(1)}, bf16[4,32,128]{2,1,0:T(8,128)(2,1)S(1)}, u32[]{:S(2)}, u32[]{:S(2)}) collective-permute-start(bf16[4,32,128]{2,1,0:T(8,128)(2,1)S(1)} %get-tuple-element.322), channel_id=1, source_target_pairs={{0,1},{1,2},{2,3},{3,4},{4,5},{5,6},{6,7},{8,9},{9,10},{10,11},{11... | collective-permute-start | bytes 98312 | tf_op jit(solution)/shard_map/ppermute | solution.py:64
  70.0 10.6 %collective-permute-start.3 = (bf16[4,32,128]{2,1,0:T(8,128)(2,1)S(1)}, bf16[4,32,128]{2,1,0:T(8,128)(2,1)S(1)}, u32[]{:S(2)}, u32[]{:S(2)}) collective-permute-start(bf16[4,32,128]{2,1,0:T(8,128)(2,1)S(1)} %get-tuple-element.323), channel_id=1, source_target_pairs={{1,0},{2,1},{3,2},{4,3},{5,4},{6,5},{7,6},{9,8},{10,9},{11,10},{12... | collective-permute-start | bytes 98312 | tf_op jit(solution)/shard_map/ppermute | solution.py:67
  73.1 4.1 %copy-start.16 = (s32[8,3]{0,1:T(4,128)S(1)}, s32[8,3]{0,1:T(4,128)}, u32[]{:S(2)}) copy-start(s32[8,3]{0,1:T(4,128)} %param.22) | copy-start | bytes 292
  73.1 8.4 %collective-permute-start = (bf16[1,32,128]{2,1,0:T(8,128)(2,1)S(1)}, bf16[1,32,128]{2,1,0:T(8,128)(2,1)S(1)}, u32[]{:S(2)}, u32[]{:S(2)}) collective-permute-start(bf16[1,32,128]{2,1,0:T(8,128)(2,1)S(1)} %get-tuple-element.320), channel_id=1, source_target_pairs={{0,8},{8,16},{16,24},{1,9},{9,17},{17,25},{2,10},{10,18},{18,26},{... | collective-permute-start | bytes 24584 | tf_op jit(solution)/shard_map/ppermute | solution.py:64
  77.1 0.7 copy-start.19
where the time goes:
time: 83.1 us; the launch traced here: 82.4 us
  matrix products  24.4 us (29%)
  blocking collectives  21.8 us (26%)
  local copies, waits for them, and re-layouts  18 us (22%)
  starting transfers between devices  12.3 us (15%)
  other arithmetic  4.47 us (5%)
  between operations  1.24 us (1%)
    unnamed x61, local copies, waits for them, and re-layouts  13.5 us
    all_gather x2, blocking collectives, prefix_2(): lax.all_gather(part.astype(kind), axis)  11.2 us
    all_gather x2, blocking collectives, entering(): lax.all_gather(part.astype(kind), axis)  10.6 us
    ppermute x2, starting transfers between devices, extended(): lax.ppermute(lax.slice_in_dim(block, block.shape[dim] - width, None, axis...  7.15 us
    dot_general x8, matrix products, solve_down(): result = jnp.dot(gap, inverse[position], preferred_element_type=jnp.float32)  7.13 us
    dot_general x14, matrix products, select_rows(): jnp.einsum('sr,rqb->sqb', weights, candidates, preferred_element_type=jnp...  6.49 us
    ppermute x2, starting transfers between devices, extended(): lax.ppermute(lax.slice_in_dim(block, 0, width, axis=dim), axis, backward)  5.14 us
    dot_general x8, matrix products, solve_up(): jnp.dot(summed.astype(jnp.bfloat16), inverse[position], preferred_element...  4.38 us
  transfers between devices with their start and end apart: 4, of which 0 were waited for; matrix products, arithmetic and copies ran while one was open for 4% of the time, Pallas kernels for 0%

commit v1 on v0

v1 whole, which is shorter than its diff:
```python
import jax
import jax.numpy as jnp
from jax import lax
from jax.experimental import pallas as pl
from jax.experimental.pallas import tpu as pltpu
from jax.sharding import PartitionSpec as P

RIM = 4

VMEM = pl.BlockSpec(memory_space=pltpu.VMEM)
SMEM = pl.BlockSpec(memory_space=pltpu.SMEM)


def mul(a, b):
    return jnp.dot(a, b, preferred_element_type=jnp.float32)


def narrow(a):
    return a.astype(jnp.bfloat16)


def sweep_kernel(
    rhs, inverse, lower, upper, lower_at, upper_at, base, response, payload, low, upp, down, exact
):
    rows, count, width = rhs.shape
    slots = lower.shape[1]
    upper_slots = upper.shape[1]
    near = count + width
    last = rows - 1
    eye = narrow(
        lax.broadcasted_iota(jnp.int32, (width, width), 0)
        == lax.broadcasted_iota(jnp.int32, (width, width), 1)
    )
    scaled = []
    for k in range(rows):
        own = inverse[k]
        scaled.append(mul(narrow(rhs[k]), own))
        low[k] = narrow(mul(lower[k].reshape(slots * width, width), own))
        upp[k] = narrow(mul(upper[k].reshape(upper_slots * width, width), own))
    down[:, :count] = jnp.zeros((rows, count, width), jnp.bfloat16)
    response[:, :near] = jnp.zeros((rows, near, width), jnp.bfloat16)
    for k in range(rows):
        down[k, count:] = eye
        response[k, near:] = eye

    for k in range(rows):
        if k == 0:
            total = low[k, :width].astype(jnp.float32)
            for m in range(1, slots):
                total = total + low[k, m * width : (m + 1) * width].astype(jnp.float32)
            exact[k, :count] = scaled[k]
            exact[k, count:] = -total
        else:
            source = jnp.concatenate([down[lower_at[k, m]] for m in range(1, slots)], axis=1)
            summed = mul(source, low[k, width:])
            exact[k, :count] = scaled[k] - summed[:count]
            exact[k, count:] = -low[k, :width].astype(jnp.float32) - summed[count:]
        down[k] = narrow(exact[k])

    for k in range(last, -1, -1):
        if k == last:
            total = upp[k, :width].astype(jnp.float32)
            for m in range(1, upper_slots):
                total = total + upp[k, m * width : (m + 1) * width].astype(jnp.float32)
            base[k] = exact[k, :count]
            response[k, :near] = narrow(exact[k])
            response[k, near:] = narrow(-total)
        else:
            source = jnp.concatenate(
                [response[upper_at[k, m]] for m in range(1, upper_slots)], axis=1
            )
            summed = mul(source, upp[k, width:])
            solved = exact[k] - summed[:near]
            base[k] = solved[:count]
            response[k, :near] = narrow(solved)
            response[k, near:] = narrow(-upp[k, :width].astype(jnp.float32) - summed[near:])

    far = near + width
    payload[:near] = down[last]
    payload[near : near + far] = response[0]
    payload[near + far :] = response[last, near:]


def chain_kernel(groups, axes, gathered, base, response, solution, rounded, ends, flow):
    rows, count, width = base.shape
    near = count + width
    far = near + width
    me = lax.axis_index(axes[0])
    side = lax.rem(lax.axis_index(axes[1]), 2)
    zero = jnp.zeros((count, width), jnp.bfloat16)

    inflow = [zero]
    for t in range(1, groups):
        add = gathered[t - 1, :count].astype(jnp.float32)
        if t > 1:
            add = add + mul(inflow[-1], gathered[t - 1, count:near])
        inflow.append(narrow(add))
    outflow = [zero]
    for t in range(groups - 1, 0, -1):
        add = gathered[t, near : near + count].astype(jnp.float32)
        add = add + mul(inflow[t], gathered[t, near + count : 2 * near])
        if t < groups - 1:
            add = add + mul(outflow[0], gathered[t, 2 * near : near + far])
        outflow.insert(0, narrow(add))
    for t in range(groups):
        flow[0, t] = inflow[t]
        flow[1, t] = outflow[t]

    both = jnp.concatenate([flow[0, me], flow[1, me]], axis=1)
    for k in range(rows):
        value = base[k] + mul(both, response[k, count:])
        solution[k] = value
        rounded[k] = narrow(value)
    rounded[rows + 1] = flow[1, me]
    prior = lax.max(me - 1, 0)
    before = flow[0, me].astype(jnp.float32) + mul(flow[1, prior], gathered[prior, near + far :])
    rounded[rows] = narrow(jnp.where(me > 0, before, 0.0))
    rim = ends.shape[1]
    for e in range(rim):
        ends[0, e] = rounded[(1 - side) * (rows - rim) + e]
        ends[1, e] = rounded[side * (rows - rim) + e]


def local_kernel(rounded, diagonal, lower, upper, lower_at, upper_at, partial):
    rows, slots, width, _ = lower.shape
    upper_slots = upper.shape[1]
    for k in range(rows):
        total = mul(rounded[k], diagonal[k])
        source = [rounded[rows]]
        for m in range(1, slots):
            at = lower_at[k, m]
            source.append(rounded[jnp.where(at == k, rows, at)])
        total = total + mul(
            jnp.concatenate(source, axis=1), lower[k].reshape(slots * width, width)
        )
        source = [rounded[rows + 1]]
        for m in range(1, upper_slots):
            at = upper_at[k, m]
            source.append(rounded[jnp.where(at == k, rows + 1, at)])
        total = total + mul(
            jnp.concatenate(source, axis=1), upper[k].reshape(upper_slots * width, width)
        )
        partial[k] = total


def halo_kernel(axis, partial, inner, outer, halo, halo_at, product, rim_rows):
    rows, slots, width, _ = halo.shape
    rim = inner.shape[0]
    turn = rim * (1 - lax.rem(lax.axis_index(axis), 2))
    rim_rows[:rim] = inner[...]
    rim_rows[rim:] = outer[...]
    for k in range(rows):
        source = [
            rim_rows[lax.rem(halo_at[k, m] + turn, 2 * rim)] for m in range(slots)
        ]
        product[k] = partial[k] + mul(
            jnp.concatenate(source, axis=1), halo[k].reshape(slots * width, width)
        )


def swaps(block, axis, first):
    count = lax.axis_size(axis)
    pairs = []
    for low in range(first, count - 1, 2):
        pairs += [(low, low + 1), (low + 1, low)]
    return lax.ppermute(block, axis, pairs)


def on_device(
    right_sides,
    diag_inverse,
    diag_blocks,
    lower_blocks,
    upper_blocks,
    halo_blocks,
    lower_index,
    upper_index,
    halo_index,
):
    rows, count, width = right_sides.shape
    slots = lower_blocks.shape[1]
    upper_slots = upper_blocks.shape[1]
    groups = lax.axis_size("section")
    near = count + width
    far = near + width
    wide = jax.ShapeDtypeStruct((rows, count, width), jnp.float32)

    base, response, payload = pl.pallas_call(
        sweep_kernel,
        out_shape=(
            wide,
            jax.ShapeDtypeStruct((rows, far, width), jnp.bfloat16),
            jax.ShapeDtypeStruct((near + far + width, width), jnp.bfloat16),
        ),
        in_specs=[VMEM] * 4 + [SMEM] * 2,
        out_specs=(VMEM, VMEM, VMEM),
        scratch_shapes=[
            pltpu.VMEM((rows, slots * width, width), jnp.bfloat16),
            pltpu.VMEM((rows, upper_slots * width, width), jnp.bfloat16),
            pltpu.VMEM((rows, near, width), jnp.bfloat16),
            pltpu.VMEM((rows, near, width), jnp.float32),
        ],
        name="sweeps",
    )(right_sides, diag_inverse, lower_blocks, upper_blocks, lower_index, upper_index)

    gathered = lax.all_gather(payload, "section")

    def chain(*refs):
        chain_kernel(groups, ("section", "dom"), *refs)

    solution, rounded, ends = pl.pallas_call(
        chain,
        out_shape=(
            wide,
            jax.ShapeDtypeStruct((rows + 2, count, width), jnp.bfloat16),
            jax.ShapeDtypeStruct((2, RIM, count, width), jnp.bfloat16),
        ),
        in_specs=[VMEM] * 3,
        out_specs=(VMEM, VMEM, VMEM),
        scratch_shapes=[pltpu.VMEM((2, groups, count, width), jnp.bfloat16)],
        name="chain",
    )(gathered, base, response)

    inner = swaps(ends[0], "dom", 0)
    outer = swaps(ends[1], "dom", 1)

    partial = pl.pallas_call(
        local_kernel,
        out_shape=wide,
        in_specs=[VMEM] * 4 + [SMEM] * 2,
        out_specs=VMEM,
        name="local_product",
    )(rounded, diag_blocks, lower_blocks, upper_blocks, lower_index, upper_index)

    def halo(*refs):
        halo_kernel("dom", *refs)

    product = pl.pallas_call(
        halo,
        out_shape=wide,
        in_specs=[VMEM] * 4 + [SMEM],
        out_specs=VMEM,
        scratch_shapes=[pltpu.VMEM((2 * RIM, count, width), jnp.bfloat16)],
        name="halo_product",
    )(partial, inner, outer, halo_blocks, halo_index)
    return (solution, product)


def solution(mesh):
    in_specs = (
        P(("section", "dom"), None, None),
        P(("section", "dom"), None, None),
        P(("section", "dom"), None, None),
        P(("section", "dom"), None, None, None),
        P(("section", "dom"), None, None, None),
        P(("section", "dom"), None, None, None),
        P(("section", "dom"), None),
        P(("section", "dom"), None),
        P(("section", "dom"), None),
    )
    out_specs = (P(("section", "dom"), None, None), P(("section", "dom"), None, None))
    return jax.shard_map(
        on_device, mesh=mesh, in_specs=in_specs, out_specs=out_specs, check_vma=False
    )
```

time: 83.1 us -> 32.7 us (0.39)
  the two profiles are of different devices: /device:TPU:17 before, /device:TPU:10 now
where the time goes in v1:
time: 32.7 us; the launch traced here: 32.4 us
  Pallas kernels  12.9 us (39%)
  blocking collectives  9.12 us (28%)
  starting transfers between devices  4.99 us (15%)
  local copies, waits for them, and re-layouts  4.7 us (14%)
  between operations  0.67 us (2%)
    all_gather x1, blocking collectives, on_device(): gathered = lax.all_gather(payload, 'section')  9.12 us
    pallas_call x1, Pallas kernels, on_device(): pl.pallas_call(sweep_kernel, out_shape=(wide, jax.ShapeDtypeStruct((rows,...  5.44 us
    ppermute x2, starting transfers between devices, swaps(): return lax.ppermute(block, axis, pairs)  4.99 us
    unnamed x11, local copies, waits for them, and re-layouts  3.92 us
    pallas_call x1, Pallas kernels, on_device(): pl.pallas_call(chain, out_shape=(wide, jax.ShapeDtypeStruct((rows + 2, co...  2.81 us
    pallas_call x1, Pallas kernels, on_device(): pl.pallas_call(local_kernel, out_shape=wide, in_specs=[VMEM] * 4 + [SMEM]...  2.62 us
    pallas_call x1, Pallas kernels, on_device(): pl.pallas_call(halo, out_shape=wide, in_specs=[VMEM] * 4 + [SMEM], out_sp...  2.02 us
    squeeze x1, local copies, waits for them, and re-layouts, on_device(): outer = swaps(ends[1], 'dom', 1)  0.78 us
  transfers between devices with their start and end apart: 2, of which 0 were waited for; matrix products, arithmetic and copies ran while one was open for 2% of the time, Pallas kernels for 8%

profile of v1, /device:TPU:10, one launch (start us, length us, event | category | flops | bytes accessed | tf_op | source)
XLA Modules:
  0.0 32.4 jit_solution(8180456389674665466)
XLA Ops:
  0.6 0.0 copy-start.2
  0.6 1.4 %copy.11.lower_at = s32[8,3]{1,0:T(8,128)} copy(s32[8,3]{0,1:T(4,128)} %param.15) | data formatting | bytes 192 | tf_op args[6]
  2.0 0.0 copy-done.2
  2.0 0.7 %copy.12.upper_at = s32[8,3]{1,0:T(8,128)} copy(s32[8,3]{0,1:T(4,128)S(1)} %copy-done.2) | data formatting | bytes 192 | tf_op args[7]
  2.7 5.4 %sweeps.1 = (f32[8,32,128]{2,1,0:T(8,128)}, bf16[8,288,128]{2,1,0:T(8,128)(2,1)}, bf16[576,128]{1,0:T(8,128)(2,1)}) custom-call(f32[8,32,128]{2,1,0:T(8,128)} %rhs.1, bf16[8,128,128]{2,1,0:T(8,128)(2,1)} %inverse.1, bf16[8,3,128,128]{3,2,1,0:T(8,128)(2,1)} %lower.3, bf16[8,3,128,128]{3,2,1,0:T(8,128)(2,1)} %upper.3, s32[8,3]{1,0:T(8,128)} %copy.11.lower_at, ...), custom_call_target="tpu_custom_call" | custom-call | tf_op jit(solution)/shard_map/sweeps/pallas_call | solution.py:188
  8.1 9.1 %all-gather = bf16[2304,128]{1,0:T(8,128)(2,1)} all-gather(bf16[576,128]{1,0:T(8,128)(2,1)} %get-tuple-element.8), channel_id=2, replica_groups=mesh['section'=4,'dom'=8] {'section'}, dimensions={0}, use_global_device_ids=true | all-gather | bytes 737280 | tf_op jit(solution)/shard_map/all_gather | solution.py:206
  17.2 2.8 %chain.1 = (f32[8,32,128]{2,1,0:T(8,128)}, bf16[10,32,128]{2,1,0:T(8,128)(2,1)}, bf16[2,4,32,128]{3,2,1,0:T(8,128)(2,1)}) custom-call(bf16[4,576,128]{2,1,0:T(8,128)(2,1)} %bitcast.5, f32[8,32,128]{2,1,0:T(8,128)} %get-tuple-element.9.refs_1_, bf16[8,288,128]{2,1,0:T(8,128)(2,1)} %get-tuple-element.10.refs_2_), custom_call_target="tpu_custom_call" | custom-call | tf_op jit(solution)/shard_map/chain/pallas_call | solution.py:211
  20.0 0.8 %slice_bitcast_fusion = (bf16[4,32,128]{2,1,0:T(8,128)(2,1)S(1)}, bf16[4,32,128]{2,1,0:T(8,128)(2,1)S(1)}) fusion(bf16[2,4,32,128]{3,2,1,0:T(8,128)(2,1)} %get-tuple-element.13), kind=kLoop, calls=%fused_computation | loop fusion | bytes 131072 | tf_op jit(solution)/shard_map/squeeze | solution.py:225
  20.8 0.0 copy-start.3
  20.8 0.6 %collective-permute-start = (bf16[4,32,128]{2,1,0:T(8,128)(2,1)S(1)}, bf16[4,32,128]{2,1,0:T(8,128)(2,1)S(1)}, u32[]{:S(2)}, u32[]{:S(2)}) collective-permute-start(bf16[4,32,128]{2,1,0:T(8,128)(2,1)S(1)} %get-tuple-element.15), channel_id=1, source_target_pairs={{0,1},{1,0},{2,3},{3,2},{4,5},{5,4},{6,7},{7,6},{8,9},{9,8},{10,11... | collective-permute-start | bytes 98312 | tf_op jit(solution)/shard_map/ppermute | solution.py:166
  21.4 4.4 %collective-permute-start.1 = (bf16[4,32,128]{2,1,0:T(8,128)(2,1)S(1)}, bf16[4,32,128]{2,1,0:T(8,128)(2,1)S(1)}, u32[]{:S(2)}, u32[]{:S(2)}) collective-permute-start(bf16[4,32,128]{2,1,0:T(8,128)(2,1)S(1)} %get-tuple-element.14), channel_id=1, source_target_pairs={{1,2},{2,1},{3,4},{4,3},{5,6},{6,5},{9,10},{10,9},{11,12},{12,11},... | collective-permute-start | bytes 98312 | tf_op jit(solution)/shard_map/ppermute | solution.py:166
  25.8 0.0 copy-done.3
  25.8 0.7 %copy.15.refs_4_ = s32[8,2]{1,0:T(8,128)} copy(s32[8,2]{0,1:T(2,128)S(1)} %copy-done.3) | data formatting | bytes 128 | tf_op args[8]
  26.5 2.6 %local_product.1.refs_0_ = f32[8,32,128]{2,1,0:T(8,128)} custom-call(bf16[10,32,128]{2,1,0:T(8,128)(2,1)} %get-tuple-element.12.rounded, bf16[8,128,128]{2,1,0:T(8,128)(2,1)} %diagonal.1, bf16[8,3,128,128]{3,2,1,0:T(8,128)(2,1)} %lower.3, bf16[8,3,128,128]{3,2,1,0:T(8,128)(2,1)} %upper.3, s32[8,3]{1,0:T(8,128)} %copy.11.lower_at, s32[8,3]{1,0:T(8,128)} %copy.12.upper_at), custom_call_target="tpu_custom_call" | custom-call | tf_op jit(solution)/shard_map/local_product/pallas_call | solution.py:227
  29.1 0.0 collective-permute-done.refs_1_
  29.1 0.0 copy-start
  29.1 0.0 collective-permute-done.1.refs_2_
  29.1 0.6 %copy-done = bf16[4,32,128]{2,1,0:T(8,128)(2,1)} copy-done((bf16[4,32,128]{2,1,0:T(8,128)(2,1)}, bf16[4,32,128]{2,1,0:T(8,128)(2,1)S(1)}, u32[]{:S(2)}) %copy-start) | copy-done | bytes 32792
  29.7 0.0 copy-start.1
  29.7 0.6 %copy-done.1 = bf16[4,32,128]{2,1,0:T(8,128)(2,1)} copy-done((bf16[4,32,128]{2,1,0:T(8,128)(2,1)}, bf16[4,32,128]{2,1,0:T(8,128)(2,1)S(1)}, u32[]{:S(2)}) %copy-start.1) | copy-done | bytes 32792
  30.3 2.0 %halo_product.1 = f32[8,32,128]{2,1,0:T(8,128)} custom-call(f32[8,32,128]{2,1,0:T(8,128)} %local_product.1.refs_0_, bf16[4,32,128]{2,1,0:T(8,128)(2,1)} %copy-done, bf16[4,32,128]{2,1,0:T(8,128)(2,1)} %copy-done.1, bf16[8,2,128,128]{3,2,1,0:T(8,128)(2,1)} %refs_3_.1, s32[8,2]{1,0:T(8,128)} %copy.15.refs_4_), custom_call_target="tpu_custom_call" | custom-call | tf_op jit(solution)/shard_map/halo_product/pallas_call | solution.py:238
Async XLA Ops:
  0.6 1.4 %copy-start.2 = (s32[8,3]{0,1:T(4,128)S(1)}, s32[8,3]{0,1:T(4,128)}, u32[]{:S(2)}) copy-start(s32[8,3]{0,1:T(4,128)} %param.16) | copy-start | bytes 292
  20.8 5.0 %copy-start.3 = (s32[8,2]{0,1:T(2,128)S(1)}, s32[8,2]{0,1:T(2,128)}, u32[]{:S(2)}) copy-start(s32[8,2]{0,1:T(2,128)} %param.17) | copy-start | bytes 196
  20.8 8.3 %collective-permute-start = (bf16[4,32,128]{2,1,0:T(8,128)(2,1)S(1)}, bf16[4,32,128]{2,1,0:T(8,128)(2,1)S(1)}, u32[]{:S(2)}, u32[]{:S(2)}) collective-permute-start(bf16[4,32,128]{2,1,0:T(8,128)(2,1)S(1)} %get-tuple-element.15), channel_id=1, source_target_pairs={{0,1},{1,0},{2,3},{3,2},{4,5},{5,4},{6,7},{7,6},{8,9},{9,8},{10,11... | collective-permute-start | bytes 98312 | tf_op jit(solution)/shard_map/ppermute | solution.py:166
  21.4 7.7 %collective-permute-start.1 = (bf16[4,32,128]{2,1,0:T(8,128)(2,1)S(1)}, bf16[4,32,128]{2,1,0:T(8,128)(2,1)S(1)}, u32[]{:S(2)}, u32[]{:S(2)}) collective-permute-start(bf16[4,32,128]{2,1,0:T(8,128)(2,1)S(1)} %get-tuple-element.14), channel_id=1, source_target_pairs={{1,2},{2,1},{3,4},{4,3},{5,6},{6,5},{9,10},{10,9},{11,12},{12,11},... | collective-permute-start | bytes 98312 | tf_op jit(solution)/shard_map/ppermute | solution.py:166
  29.1 0.6 %copy-start = (bf16[4,32,128]{2,1,0:T(8,128)(2,1)}, bf16[4,32,128]{2,1,0:T(8,128)(2,1)S(1)}, u32[]{:S(2)}) copy-start(bf16[4,32,128]{2,1,0:T(8,128)(2,1)S(1)} %collective-permute-done.refs_1_) | copy-start | bytes 98308
  29.7 0.6 %copy-start.1 = (bf16[4,32,128]{2,1,0:T(8,128)(2,1)}, bf16[4,32,128]{2,1,0:T(8,128)(2,1)S(1)}, u32[]{:S(2)}) copy-start(bf16[4,32,128]{2,1,0:T(8,128)(2,1)S(1)} %collective-permute-done.1.refs_2_) | copy-start | bytes 98308
